TPU v7x, 128 devices: a whole 4x4x4 slice. The times are simulated.
128 devices in a mesh: tm: 16 (over z, x_lo, core), inp: 8 (over y, x_hi).
Axes of the slice: x: 4 (x_hi: 2, x_lo: 2; x = x_hi * 2 + x_lo), y: 4, z: 4, core: 2. Of those that a mesh axis runs over, the one named last changes fastest.
Arguments:
- voltages: bfloat16 [512, 2097152], P('inp', 'tm'), may hold values from -6 to 6
- taps: float32 [8, 16384], replicated, may hold values from -2 to 2
Outputs:
- visibility: float32 [512, 2, 512, 512], P(('tm', 'inp'))
All inputs are finite; a program needn't handle non-finite values.
Results may differ from a plain program's by a relative error of at most 0.0059.
Values may be sent and summed in bfloat16 or wider, within the bound.
No kernel may reach another device: no remote copies, remote signals or barrier semaphores. Data moves between devices by JAX's collectives and lax.ppermute only.
A program may use at most 256 MiB of HBM per device.

v0:
```python
import math

import jax
import jax.numpy as jnp
from jax import lax
from jax.sharding import PartitionSpec as P

CH = 512
START = 1024


def shifted(value, axis, steps):
    count = lax.axis_size(axis)
    leading, last = (max(0, -steps), min(count, count - steps))
    return lax.ppermute(value, axis, [(source, source + steps) for source in range(leading, last)])


def dft_table(frame_len, first, count):
    rows_idx = jnp.arange(frame_len, dtype=jnp.int32)[:, None]
    cols_idx = (jnp.arange(count, dtype=jnp.int32) + first)[None, :]
    phase = rows_idx * cols_idx % frame_len
    angle = phase.astype(jnp.float32) * jnp.float32(2.0 * math.pi / frame_len)
    return jnp.concatenate([jnp.cos(angle), -jnp.sin(angle)], axis=1).astype(jnp.bfloat16)


def correlate(block, tm_count, inp_count, frames_dev, in_dev):
    items = block.shape[2]
    inputs_all = inp_count * in_dev
    total_frames = tm_count * frames_dev
    grid = block.reshape(2, tm_count, inp_count, items, frames_dev, in_dev)
    grid = jnp.transpose(grid, (3, 0, 2, 5, 1, 4)).reshape(items, 2 * inputs_all, total_frames)

    def one_channel(stacked):
        product = jnp.dot(stacked, stacked.T, preferred_element_type=jnp.float32)
        real_part = product[:inputs_all, :inputs_all] + product[inputs_all:, inputs_all:]
        imag_part = product[inputs_all:, :inputs_all] - product[:inputs_all, inputs_all:]
        return jnp.stack([real_part, imag_part]) / jnp.float32(total_frames)

    return lax.map(one_channel, grid)


def on_device(voltages, taps):
    in_dev, samples = voltages.shape
    tap_count, frame_len = taps.shape
    frames_dev = samples // frame_len
    blocks = voltages.reshape(in_dev, frames_dev, frame_len)
    history = shifted(blocks[:, frames_dev - tap_count + 1 :, :], "tm", 1)
    extended = jnp.concatenate([history, blocks], axis=1)
    filtered = jnp.zeros((in_dev, frames_dev, frame_len), jnp.float32)
    for tap in range(tap_count):
        start = tap_count - 1 - tap
        filtered = filtered + taps[tap][None, None, :] * extended[
            :, start : start + frames_dev, :
        ].astype(jnp.float32)
    filtered = filtered.astype(jnp.bfloat16)
    flat_rows = jnp.transpose(filtered, (1, 0, 2)).reshape(frames_dev * in_dev, frame_len)
    table = dft_table(frame_len, START, CH)
    spectra = lax.dot_general(
        table, flat_rows, (((0,), (1,)), ((), ())), preferred_element_type=jnp.float32
    )
    spectra = (spectra * jnp.float32(1.0 / math.sqrt(frame_len))).astype(jnp.bfloat16)
    tm_count = lax.axis_size("tm")
    inp_count = lax.axis_size("inp")
    device_count = tm_count * inp_count
    per_device = CH // device_count
    row_width = frames_dev * in_dev
    payload = spectra.reshape(2, device_count, 1, per_device, row_width)
    return correlate(
        lax.all_to_all(payload, ("tm", "inp"), split_axis=1, concat_axis=2, tiled=True)[:, 0],
        tm_count,
        inp_count,
        frames_dev,
        in_dev,
    )


def solution(mesh):
    return jax.shard_map(
        on_device,
        mesh=mesh,
        in_specs=(P("inp", "tm"), P()),
        out_specs=P(("tm", "inp"), None, None, None),
        check_vma=False,
    )
```

profile of v0, /device:TPU:1, one launch (start us, length us, event | category | flops | bytes accessed | tf_op | source)
XLA Modules:
  0.0 417.8 jit_solution(9765921144270700812)
XLA Ops:
  0.0 14.7 %copy.17 = bf16[8,8,8,16384]{3,2,1,0:T(8,128)(2,1)S(1)} copy(bf16[8,8,8,16384]{3,1,2,0:T(8,128)(2,1)} %bitcast.38) | data formatting | bytes 33554432
  14.7 3.9 slice.80
  18.6 1.8 copy-done
  20.4 18.7 %copy.9 = bf16[64,7,16384]{2,0,1:T(8,128)(2,1)} copy(bf16[64,7,16384]{2,1,0:T(8,128)(2,1)S(1)} %slice.80) | data formatting | bytes 29360128 | tf_op jit(solution)/shard_map/slice | solution.py:47
  39.1 4.7 %collective-permute-start = (bf16[64,7,16384]{2,0,1:T(8,128)(2,1)}, bf16[64,7,16384]{2,0,1:T(8,128)(2,1)S(1)}, u32[]{:S(2)}, u32[]{:S(2)}) collective-permute-start(bf16[64,7,16384]{2,0,1:T(8,128)(2,1)} %copy.9), channel_id=1, source_target_pairs={{0,8},{8,16},{16,24},{24,32},{32,40},{40,48},{48,56},{56,64},{64,7... | collective-permute-start | bytes 44040200 | tf_op jit(solution)/shard_map/ppermute | solution.py:15
  43.8 0.4 fusion.27
  44.2 136.1 %cosine_convert_fusion = (bf16[16384,512]{1,0:T(8,128)(2,1)}, bf16[16384,512]{1,0:T(8,128)(2,1)}) fusion(s32[512]{0:T(512)S(1)} %iota_add_fusion), kind=kLoop, calls=%fused_computation.34 | loop fusion | flops 142606336 | bytes 33556480 | tf_op jit(solution)/shard_map/convert
  180.3 21.5 %collective-permute-done = bf16[64,7,16384]{2,0,1:T(8,128)(2,1)S(1)} collective-permute-done((bf16[64,7,16384]{2,0,1:T(8,128)(2,1)}, bf16[64,7,16384]{2,0,1:T(8,128)(2,1)S(1)}, u32[]{:S(2)}, u32[]{:S(2)}) %collective-permute-start) | collective-permute-done | bytes 14680096 | tf_op jit(solution)/shard_map/ppermute | solution.py:15
  201.7 22.4 %copy.10 = bf16[64,7,16384]{2,1,0:T(8,128)(2,1)} copy(bf16[64,7,16384]{2,0,1:T(8,128)(2,1)S(1)} %collective-permute-done) | data formatting | bytes 29360128 | tf_op jit(solution)/shard_map/ppermute | solution.py:15
  224.1 101.0 %fusion.23 = bf16[8,64,16384]{2,0,1:T(8,128)(2,1)} fusion(bf16[64,8,16384]{2,1,0:T(8,128)(2,1)} %bitcast.37, bf16[64,7,16384]{2,1,0:T(8,128)(2,1)} %copy.10, f32[16384]{0:T(1024)S(1)} %bitcast.47, f32[16384]{0:T(1024)S(1)} %bitcast.48, f32[16384]{0:T(1024)S(1)} %bitcast.42, f32[16384]{0:T(1024)S(1)} %bitcast.43, f32[16384]{0:T(1024)S(1)} %bitcast.44, ...), kind=kLoop, calls=%fused_computation.45 | loop fusion | flops 377487360 | bytes 48758784 | tf_op jit(solution)/shard_map/transpose | solution.py:56
  325.1 18.5 %copy.11 = bf16[8,64,16384]{2,1,0:T(8,128)(2,1)} copy(bf16[8,64,16384]{2,0,1:T(8,128)(2,1)} %fusion.23) | data formatting | bytes 33554432 | tf_op jit(solution)/shard_map/transpose | solution.py:56
  343.6 23.2 %multiply_convert_fusion = bf16[1024,512]{1,0:T(8,128)(2,1)S(1)} fusion(bf16[512,16384]{1,0:T(8,128)(2,1)} %bitcast.39, bf16[16384,512]{1,0:T(8,128)(2,1)} %get-tuple-element.49, bf16[16384,512]{1,0:T(8,128)(2,1)} %get-tuple-element.48), kind=kOutput, calls=%fused_computation.46 | convolution fusion | flops 17248026624 | bytes 51380224 | tf_op jit(solution)/shard_map/dot_general | solution.py:58
  367.1 1.3 copy.12
  368.4 12.2 %all-to-all-start = ((bf16[2,128,1,4,512]{4,3,0,2,1:T(4,128)(2,1)}), bf16[2,128,1,4,512]{4,3,0,2,1:T(4,128)(2,1)S(1)}, u32[]{:S(2)}, u32[]{:S(2)}) async-start(bf16[2,128,1,4,512]{4,3,0,2,1:T(4,128)(2,1)} %copy.12), calls=%async_computation | async-start | bytes 2097152 | tf_op jit(solution)/shard_map/all_to_all | solution.py:69
  380.6 19.5 %all-to-all-done = bf16[2,128,1,4,512]{4,3,0,2,1:T(4,128)(2,1)S(1)} async-done(((bf16[2,128,1,4,512]{4,3,0,2,1:T(4,128)(2,1)}), bf16[2,128,1,4,512]{4,3,0,2,1:T(4,128)(2,1)S(1)}, u32[]{:S(2)}, u32[]{:S(2)}) %all-to-all-start) | async-done | bytes 1048608 | tf_op jit(solution)/shard_map/all_to_all | solution.py:69
  400.1 0.3 copy.13
  400.4 1.1 reshape_squeeze.3
  401.5 2.0 copy.14
  403.5 3.2 reshape.62
  406.7 11.1 %while.10 = (s32[]{:T(128)}, f32[4,2,512,512]{3,2,1,0:T(8,128)}, bf16[4,1024,128]{1,2,0:T(8,128)(2,1)S(1)}, s32[]{:T(128)}) while((s32[]{:T(128)}, f32[4,2,512,512]{3,2,1,0:T(8,128)}, bf16[4,1024,128]{1,2,0:T(8,128)(2,1)S(1)}, s32[]{:T(128)}) %tuple.32), condition=%wide.region_1.2_spmd, body=%wide.region_0.1_spmd.sunk | while | flops 270008320 | bytes 14942777 | solution.py:39
  406.7 0.7 fusion.34
  407.5 0.5 fusion.35
  408.0 1.6 fusion.36
  409.5 0.7 fusion.34
  410.2 0.5 fusion.35
  410.7 1.6 fusion.36
  412.3 0.7 fusion.34
  413.0 0.5 fusion.35
  413.5 1.6 fusion.36
  415.1 0.7 fusion.34
  415.8 0.5 fusion.35
  416.3 1.6 fusion.36
  (6 shorter events, 0.3 us)
Async XLA Ops:
  14.7 5.7 %copy-start = (bf16[8,8,8,16384]{3,2,1,0:T(8,128)(2,1)}, bf16[8,8,8,16384]{3,2,1,0:T(8,128)(2,1)S(1)}, u32[]{:S(2)}) copy-start(bf16[8,8,8,16384]{3,2,1,0:T(8,128)(2,1)S(1)} %copy.17) | copy-start | bytes 50331652
  20.4 23.4 %copy-start.1 = (f32[8,16384]{1,0:T(8,128)S(1)}, f32[8,16384]{1,0:T(8,128)}, u32[]{:S(2)}) copy-start(f32[8,16384]{1,0:T(8,128)} %param.5) | copy-start | bytes 1572868
  39.1 162.6 %collective-permute-start = (bf16[64,7,16384]{2,0,1:T(8,128)(2,1)}, bf16[64,7,16384]{2,0,1:T(8,128)(2,1)S(1)}, u32[]{:S(2)}, u32[]{:S(2)}) collective-permute-start(bf16[64,7,16384]{2,0,1:T(8,128)(2,1)} %copy.9), channel_id=1, source_target_pairs={{0,8},{8,16},{16,24},{24,32},{32,40},{40,48},{48,56},{56,64},{64,7... | collective-permute-start | bytes 44040200 | tf_op jit(solution)/shard_map/ppermute | solution.py:15
  368.4 31.7 %all-to-all-start = ((bf16[2,128,1,4,512]{4,3,0,2,1:T(4,128)(2,1)}), bf16[2,128,1,4,512]{4,3,0,2,1:T(4,128)(2,1)S(1)}, u32[]{:S(2)}, u32[]{:S(2)}) async-start(bf16[2,128,1,4,512]{4,3,0,2,1:T(4,128)(2,1)} %copy.12), calls=%async_computation | async-start | bytes 2097152 | tf_op jit(solution)/shard_map/all_to_all | solution.py:69
where the time goes:
time: 418 us
  other arithmetic  245 us (59%)
  local copies, waits for them, and re-layouts  88.6 us (21%)
  waiting for transfers between devices  41 us (10%)
  matrix products  26.1 us (6%)
  starting transfers between devices  16.8 us (4%)
    another operation x1, other arithmetic  136 us
    transpose x1, other arithmetic, on_device(): jnp.transpose(filtered, (1, 0, 2)).reshape(frames_dev * in_dev, frame_len)  101 us
    dot_general x1, matrix products, on_device(): lax.dot_general(table, flat_rows, (((0,), (1,)), ((), ())), preferred_ele...  23.2 us
    slice x2, local copies, waits for them, and re-layouts, on_device(): history = shifted(blocks[:, frames_dev - tap_count + 1:, :], 'tm', 1)  22.6 us
    ppermute x1, local copies, waits for them, and re-layouts, shifted(): lax.ppermute(value, axis, [(source, source + steps) for source in range(l...  22.4 us
    ppermute x1, waiting for transfers between devices, shifted(): lax.ppermute(value, axis, [(source, source + steps) for source in range(l...  21.5 us
    all_to_all x1, waiting for transfers between devices, on_device(): lax.all_to_all(payload, ('tm', 'inp'), split_axis=1, concat_axis=2, tiled...  19.5 us
    transpose x1, local copies, waits for them, and re-layouts, on_device(): jnp.transpose(filtered, (1, 0, 2)).reshape(frames_dev * in_dev, frame_len)  18.5 us
  transfers between devices with their start and end apart: 2, of which 2 were waited for; matrix products, arithmetic and copies ran while one was open for 33% of the time, Pallas kernels for 0%

commit v1 on v0

v1 whole, which is shorter than its diff:
```python
import functools
import math

import jax
import jax.numpy as jnp
from jax import lax
from jax.experimental import pallas as pl
from jax.experimental.pallas import tpu as pltpu
from jax.sharding import PartitionSpec as P

CH = 512
START = 1024
RADIX = 4
LANES = 128
NT = (((1,), (1,)), ((), ()))
TN = (((0,), (0,)), ((), ()))
PLACES = ((0, 1), (4, 6), (2, 3), (7, 5))


def unit_roots(phase, frame_len):
    angle = (phase % frame_len).astype(jnp.float32) * jnp.float32(2.0 * math.pi / frame_len)
    return jnp.cos(angle), jnp.sin(angle)


def table_kernel(groups, step_cos, step_sin, first_cos, first_sin, coarse_cos, coarse_sin, out, fine_cos, fine_sin):
    quarter = step_cos.shape[0]

    @pl.when(pl.program_id(0) == 0)
    def _():
        for res in range(RADIX):
            c0, s0 = step_cos[...], step_sin[...]
            c1, s1 = first_cos[res : res + 1, :], first_sin[res : res + 1, :]
            fine_cos[res] = c0 * c1 - s0 * s1
            fine_sin[res] = s0 * c1 + c0 * s1

    for group in range(groups):
        lanes = slice(group * LANES, (group + 1) * LANES)
        for res in range(RADIX):
            rows = slice(res * quarter, (res + 1) * quarter)
            c0, s0 = fine_cos[res], fine_sin[res]
            c1, s1 = coarse_cos[0, rows, group : group + 1], coarse_sin[0, rows, group : group + 1]
            cosine, sine = PLACES[res]
            out[cosine * quarter : (cosine + 1) * quarter, lanes] = (c0 * c1 - s0 * s1).astype(jnp.bfloat16)
            out[sine * quarter : (sine + 1) * quarter, lanes] = (-s0 * c1 - c0 * s1).astype(jnp.bfloat16)


def twiddles(frame_len, groups=4):
    span = frame_len // RADIX
    quarter = CH // RADIX
    steps = span // (LANES * groups)
    columns = jnp.arange(LANES, dtype=jnp.int32)[None, :]
    offsets = jnp.arange(quarter, dtype=jnp.int32)[:, None]
    step = unit_roots(RADIX * offsets * columns, frame_len)
    first = unit_roots((START + jnp.arange(8, dtype=jnp.int32)[:, None]) * columns, frame_len)
    channels = START + jnp.arange(RADIX, dtype=jnp.int32)[:, None, None] + RADIX * offsets[None]
    blocks = LANES * jnp.arange(span // LANES, dtype=jnp.int32)
    coarse = unit_roots(channels.reshape(CH, 1) * blocks[None, :], frame_len)
    coarse = lax.optimization_barrier(coarse)
    coarse = [jnp.transpose(part.reshape(CH, steps, groups), (1, 0, 2)) for part in coarse]
    return pl.pallas_call(
        functools.partial(table_kernel, groups),
        grid=(steps,),
        in_specs=[pl.BlockSpec((quarter, LANES), lambda i: (0, 0))] * 2
        + [pl.BlockSpec((8, LANES), lambda i: (0, 0))] * 2
        + [pl.BlockSpec((1, CH, groups), lambda i: (i, 0, 0))] * 2,
        out_specs=pl.BlockSpec((2 * CH, groups * LANES), lambda i: (0, i)),
        out_shape=jax.ShapeDtypeStruct((2 * CH, span), jnp.bfloat16),
        scratch_shapes=[pltpu.VMEM((RADIX, quarter, LANES), jnp.float32)] * 2,
        name="twiddles",
    )(*step, *first, *coarse)


def spectra_kernel(tail, frames, width, samples, taps, table, out, parts, sums_ref, stage):
    step = pl.program_id(0)
    taps_count = taps.shape[1]
    groups, low = samples.shape[0], samples.shape[2]
    in_dev = groups * low
    made = taps_count - 1 if tail else frames
    columns = frames * in_dev

    @pl.when(step == 0)
    def _():
        sums_ref[...] = jnp.zeros_like(sums_ref)
        if tail:
            parts[...] = jnp.zeros_like(parts)

    for lane in range(width // LANES):
        lanes = slice(lane * LANES, (lane + 1) * LANES)
        for group in range(groups):
            block = [
                [samples[group, n * RADIX + b, :, lanes].astype(jnp.float32) for n in range(frames)]
                for b in range(RADIX)
            ]
            for m in range(made):
                quad = []
                for b in range(RADIX):
                    total = None
                    for t in range(taps_count):
                        n = frames + m - t if tail else m - t
                        if 0 <= n < frames:
                            term = taps[b, t : t + 1, lanes] * block[b][n]
                            total = term if total is None else total + term
                    quad.append(total)
                s02, d02 = quad[0] + quad[2], quad[0] - quad[2]
                s13, d13 = quad[1] + quad[3], quad[1] - quad[3]
                start = m * in_dev + group * low
                rows = slice(start, start + low)
                parts[0, rows, lanes] = s02 + s13
                parts[1, rows, lanes] = s02 - s13
                parts[2, rows, lanes] = d02
                parts[3, rows, lanes] = d13

    quarter = table.shape[0] // (2 * RADIX)

    def product(block, part, negative=False):
        rows = table[2 * block * quarter : 2 * (block + 1) * quarter, :]
        rows = -rows if negative else rows
        return lax.dot_general(rows, parts[part], NT, preferred_element_type=jnp.float32)

    sums_ref[0] += product(0, 0)
    sums_ref[1] += product(1, 1)
    sums_ref[2] += product(2, 2) + product(3, 3)
    sums_ref[3] += product(3, 2) + product(2, 3, True)

    @pl.when(step == pl.num_programs(0) - 1)
    def _():
        scale = jnp.float32(1.0 / math.sqrt(RADIX * width * pl.num_programs(0)))
        tiles = columns // LANES
        height = 2 * RADIX * tiles
        target = stage if tail else out
        for place, (block, part) in enumerate(((0, 0), (0, 1), (2, 0), (3, 0), (1, 0), (1, 1), (3, 1), (2, 1))):
            for tile in range(tiles):
                target[pl.ds(place * tiles + tile, quarter, stride=height), :] = (
                    sums_ref[block, part * quarter : (part + 1) * quarter, tile * LANES : (tile + 1) * LANES]
                    * scale
                )
        if tail:
            out[...] = stage[...].astype(out.dtype)


def frame_spectra(voltages, taps, table, tail, width=512):
    in_dev, length = voltages.shape
    tap_count, frame_len = taps.shape
    frames = length // frame_len
    span = frame_len // RADIX
    quarter = CH // RADIX
    columns = frames * in_dev

    low = 8
    samples = voltages.reshape(in_dev // low, low, frames * RADIX, span)
    samples = jnp.transpose(samples, (0, 2, 1, 3))
    taps = jnp.transpose(taps.reshape(tap_count, RADIX, span), (1, 0, 2))
    in_specs = [
        pl.BlockSpec((in_dev // low, frames * RADIX, low, width), lambda i: (0, 0, 0, i)),
        pl.BlockSpec((RADIX, tap_count, width), lambda i: (0, 0, i)),
        pl.BlockSpec((2 * CH, width), lambda i: (0, i)),
    ]
    height = quarter * 2 * RADIX * (columns // LANES)
    return pl.pallas_call(
        functools.partial(spectra_kernel, tail, frames, width),
        grid=(span // width,),
        in_specs=in_specs,
        out_specs=pl.BlockSpec((height, LANES), lambda i: (0, 0)),
        out_shape=jax.ShapeDtypeStruct((height, LANES), jnp.bfloat16 if tail else jnp.float32),
        scratch_shapes=[
            pltpu.VMEM((RADIX, columns, width), jnp.float32),
            pltpu.VMEM((RADIX, 2 * quarter, columns), jnp.float32),
            pltpu.VMEM((height if tail else 8, LANES), jnp.float32),
        ],
        compiler_params=pltpu.CompilerParams(vmem_limit_bytes=50 * 2**20),
        cost_estimate=pl.CostEstimate(
            flops=2 * columns * 6 * quarter * 2 * span, bytes_accessed=26 * 2**20, transcendentals=0
        ),
        name="tail_spectra" if tail else "main_spectra",
    )(samples, taps, table)


def visibility_kernel(tm_count, inp_count, total_frames, block, out, left, right):
    lane = lax.broadcasted_iota(jnp.int32, (tm_count, 8, LANES), 2)
    row = lax.broadcasted_iota(jnp.int32, (tm_count, 8, LANES), 1)
    low = lane < LANES // 2
    real_row = row < 4
    half_depth = tm_count * 8
    scale = jnp.float32(1.0 / total_frames)
    for channel in range(block.shape[1] // 8):
        values = block[...].astype(jnp.float32)[:, channel * 8 : channel * 8 + 8, :]
        values = values.reshape(tm_count, inp_count, 8, LANES)
        for pair in range(inp_count // 2):
            first, second = values[:, 2 * pair], values[:, 2 * pair + 1]
            merged = (
                jnp.where(low, first, pltpu.roll(second, LANES // 2, 2)),
                jnp.where(low, pltpu.roll(first, LANES // 2, 2), second),
            )
            lanes = slice(pair * LANES, (pair + 1) * LANES)
            for part in range(2):
                rows = slice(part * half_depth, (part + 1) * half_depth)
                swapped = pltpu.roll(merged[part], 4, 1)
                swapped = jnp.where(real_row, -swapped, swapped)
                left[rows, lanes] = merged[part].reshape(half_depth, LANES).astype(jnp.bfloat16)
                right[rows, lanes] = swapped.reshape(half_depth, LANES).astype(jnp.bfloat16)
        out[channel, 0] = (
            lax.dot_general(left[...], left[...], TN, preferred_element_type=jnp.float32) * scale
        )
        out[channel, 1] = (
            lax.dot_general(left[...], right[...], TN, preferred_element_type=jnp.float32) * scale
        )


def visibilities(spectra, tm_count, inp_count, total_frames, inputs_all):
    devices, height, _ = spectra.shape
    per_device = CH // devices
    depth = 2 * tm_count * 8
    return pl.pallas_call(
        functools.partial(visibility_kernel, tm_count, inp_count, total_frames),
        grid=(height // 16,),
        in_specs=[pl.BlockSpec((devices, 16, LANES), lambda i: (0, i, 0))],
        out_specs=pl.BlockSpec((2, 2, inputs_all, inputs_all), lambda i: (i, 0, 0, 0)),
        out_shape=jax.ShapeDtypeStruct((per_device, 2, inputs_all, inputs_all), jnp.float32),
        scratch_shapes=[
            pltpu.VMEM((depth, inputs_all), jnp.bfloat16),
            pltpu.VMEM((depth, inputs_all), jnp.bfloat16),
        ],
        compiler_params=pltpu.CompilerParams(vmem_limit_bytes=50 * 2**20),
        name="visibilities",
    )(spectra)


def on_device(voltages, taps):
    in_dev, samples = voltages.shape
    frame_len = taps.shape[1]
    frames_dev = samples // frame_len
    tm_count, inp_count = lax.axis_size("tm"), lax.axis_size("inp")
    devices = tm_count * inp_count
    table = twiddles(frame_len)
    tail = frame_spectra(voltages, taps, table, True)
    tail, table, voltages = lax.optimization_barrier((tail, table, voltages))
    carried = lax.ppermute(tail, "tm", [(i, i + 1) for i in range(tm_count - 1)])
    main = frame_spectra(voltages, taps, table, False)
    spectra = (main + carried.astype(jnp.float32)).astype(jnp.bfloat16)
    spectra = spectra.reshape(devices, -1, LANES)
    spectra = lax.all_to_all(spectra, ("tm", "inp"), split_axis=0, concat_axis=0, tiled=True)
    return visibilities(spectra, tm_count, inp_count, tm_count * frames_dev, inp_count * in_dev)


def solution(mesh):
    return jax.shard_map(
        on_device,
        mesh=mesh,
        in_specs=(P("inp", "tm"), P()),
        out_specs=P(("tm", "inp"), None, None, None),
        check_vma=False,
    )
```

time: 418 us -> 100 us (0.24)
  other arithmetic: 245 us -> 2.35 us
  local copies, waits for them, and re-layouts: 88.6 us -> 3.98 us
  Pallas kernels: 0 us -> 59.6 us
  waiting for transfers between devices: 41 us -> 0.01 us
  blocking collectives: 0 us -> 29.4 us
  matrix products: 26.1 us -> 0 us
  starting transfers between devices: 16.8 us -> 4.5 us
    another operation x5 -> x0, other arithmetic: 138 us -> none
    transpose x1 -> x0, other arithmetic: 101 us -> none  [on_device(): jnp.transpose(filtered, (1, 0, 2)).reshape(frames_dev * in_dev, frame_len)]
    pallas_call x0 -> x4, Pallas kernels: none -> 59.6 us  [the longest x2 45.5 us: frame_spectra(): pl.pallas_call(functools.partial(spectra_kernel, tail, frames, width), gr...]
    all_to_all x0 -> x1, blocking collectives: none -> 29.4 us  [on_device(): lax.all_to_all(spectra, ('tm', 'inp'), split_axis=0, concat_axis=0, tiled...]
    dot_general x5 -> x0, matrix products: 26.1 us -> none  [the longest x1 23.2 us: on_device(): lax.dot_general(table, flat_rows, (((0,), (1,)), ((), ())), preferred_ele...]
    slice x3 -> x0, local copies, waits for them, and re-layouts: 23 us -> none  [the longest x2 22.6 us: on_device(): history = shifted(blocks[:, frames_dev - tap_count + 1:, :], 'tm', 1)]
    ppermute x1 -> x0, local copies, waits for them, and re-layouts: 22.4 us -> none  [shifted(): lax.ppermute(value, axis, [(source, source + steps) for source in range(l...]
    ppermute x1, waiting for transfers between devices: 21.5 us -> 0.01 us  [on_device(): lax.ppermute(tail, 'tm', [(i, i + 1) for i in range(tm_count - 1)])]
  transfers between devices with their start and end apart: 2 -> 1, of which waited for: 2 -> 0; matrix products, arithmetic and copies ran while one was open for 33% -> 0% of each run, Pallas kernels for 0% -> 24%
where the time goes in v1:
time: 100 us; the launch traced here: 99.9 us
  Pallas kernels  59.6 us (60%)
  blocking collectives  29.4 us (29%)
  starting transfers between devices  4.5 us (4%)
  local copies, waits for them, and re-layouts  3.98 us (4%)
  other arithmetic  2.35 us (2%)
    pallas_call x2, Pallas kernels, frame_spectra(): pl.pallas_call(functools.partial(spectra_kernel, tail, frames, width), gr...  45.5 us
    all_to_all x1, blocking collectives, on_device(): lax.all_to_all(spectra, ('tm', 'inp'), split_axis=0, concat_axis=0, tiled...  29.4 us
    pallas_call x1, Pallas kernels, twiddles(): pl.pallas_call(functools.partial(table_kernel, groups), grid=(steps,), in...  9.55 us
    pallas_call x1, Pallas kernels, visibilities(): pl.pallas_call(functools.partial(visibility_kernel, tm_count, inp_count,...  4.52 us
    ppermute x1, starting transfers between devices, on_device(): lax.ppermute(tail, 'tm', [(i, i + 1) for i in range(tm_count - 1)])  4.5 us
    reshape x4, local copies, waits for them, and re-layouts, twiddles(): part.reshape(CH, steps, groups)  3.98 us
    sin x3, other arithmetic, unit_roots(): return (jnp.cos(angle), jnp.sin(angle))  2.05 us
  transfers between devices with their start and end apart: 1, of which 0 were waited for; matrix products, arithmetic and copies ran while one was open for 0% of the time, Pallas kernels for 24%

profile of v1, /device:TPU:1, one launch (start us, length us, event | category | flops | bytes accessed | tf_op | source)
XLA Modules:
  0.0 99.9 jit_solution(12442289402286774081)
XLA Ops:
  0.0 0.7 fusion.19
  0.7 1.0 fusion.11
  1.7 0.1 bitcast_add_fusion
  1.8 0.3 fusion.9
  2.2 2.0 %copy.4 = f32[512,8,4]{2,0,1:T(8,128)} copy(f32[512,8,4]{0,2,1:T(4,128)S(1)} %reshape.71) | data formatting | bytes 131072 | tf_op jit(solution)/shard_map/reshape | solution.py:59
  4.2 2.0 %copy.3 = f32[512,8,4]{2,0,1:T(8,128)} copy(f32[512,8,4]{0,2,1:T(4,128)S(1)} %reshape.70) | data formatting | bytes 131072 | tf_op jit(solution)/shard_map/reshape | solution.py:59
  6.1 0.0 copy-start
  6.2 9.6 %twiddles.1.table = bf16[1024,4096]{1,0:T(8,128)(2,1)} custom-call(f32[128,128]{1,0:T(8,128)} %get-tuple-element.20.step_cos, f32[128,128]{1,0:T(8,128)} %get-tuple-element.19.step_sin, f32[8,128]{1,0:T(8,128)} %get-tuple-element.18.first_cos, f32[8,128]{1,0:T(8,128)} %get-tuple-element.17.first_sin, f32[8,512,4]{2,1,0:T(8,128)} %bitcast.24, ...), custom_call_target="tpu_custom_call" | custom-call | tf_op jit(solution)/shard_map/twiddles/pallas_call | solution.py:60
  15.7 0.0 copy-done
  15.7 21.9 %tail_spectra.1 = bf16[4096,128]{1,0:T(8,128)(2,1)S(1)} custom-call(bf16[8,32,8,4096]{3,2,1,0:T(8,128)(2,1)} %bitcast.21, f32[4,8,4096]{2,1,0:T(8,128)S(1)} %bitcast.19, bf16[1024,4096]{1,0:T(8,128)(2,1)} %twiddles.1.table), custom_call_target="tpu_custom_call" | custom-call | flops 6442450944 | bytes 27262976 | tf_op jit(solution)/shard_map/tail_spectra/pallas_call | solution.py:159
  37.6 4.5 %collective-permute-start = (bf16[4096,128]{1,0:T(8,128)(2,1)S(1)}, bf16[4096,128]{1,0:T(8,128)(2,1)S(1)}, u32[]{:S(2)}, u32[]{:S(2)}) collective-permute-start(bf16[4096,128]{1,0:T(8,128)(2,1)S(1)} %tail_spectra.1), channel_id=1, source_target_pairs={{0,8},{8,16},{16,24},{24,32},{32,40},{40,48},{48,56},{56,64},{64,7... | collective-permute-start | bytes 3145736 | tf_op jit(solution)/shard_map/ppermute | solution.py:237
  42.1 23.6 %main_spectra.1 = f32[4096,128]{1,0:T(8,128)S(1)} custom-call(bf16[8,32,8,4096]{3,2,1,0:T(8,128)(2,1)} %bitcast.22, f32[4,8,4096]{2,1,0:T(8,128)S(1)} %bitcast.20, bf16[1024,4096]{1,0:T(8,128)(2,1)} %twiddles.1.table), custom_call_target="tpu_custom_call" | custom-call | flops 6442450944 | bytes 27262976 | tf_op jit(solution)/shard_map/main_spectra/pallas_call | solution.py:159
  65.8 0.0 collective-permute-done
  65.8 0.2 add_convert_fusion
  66.0 29.4 %all_to_all.5.block = bf16[128,32,128]{2,1,0:T(8,128)(2,1)S(1)} all-to-all(bf16[128,32,128]{2,1,0:T(8,128)(2,1)S(1)} %bitcast.25), channel_id=1, replica_groups=mesh['tm'=16,'inp'=8] {'tm','inp'}, dimensions={0} | all-to-all | bytes 2097152 | tf_op jit(solution)/shard_map/all_to_all | solution.py:241
  95.4 4.5 %visibilities.1 = f32[4,2,512,512]{3,2,1,0:T(8,128)} custom-call(bf16[128,32,128]{2,1,0:T(8,128)(2,1)S(1)} %all_to_all.5.block), custom_call_target="tpu_custom_call" | custom-call | tf_op jit(solution)/shard_map/visibilities/pallas_call | solution.py:213
  (7 shorter events, 0.1 us)
Async XLA Ops:
  6.1 9.6 %copy-start = (f32[8,16384]{1,0:T(8,128)S(1)}, f32[8,16384]{1,0:T(8,128)}, u32[]{:S(2)}) copy-start(f32[8,16384]{1,0:T(8,128)} %param.3) | copy-start | bytes 1572868
  37.6 28.1 %collective-permute-start = (bf16[4096,128]{1,0:T(8,128)(2,1)S(1)}, bf16[4096,128]{1,0:T(8,128)(2,1)S(1)}, u32[]{:S(2)}, u32[]{:S(2)}) collective-permute-start(bf16[4096,128]{1,0:T(8,128)(2,1)S(1)} %tail_spectra.1), channel_id=1, source_target_pairs={{0,8},{8,16},{16,24},{24,32},{32,40},{40,48},{48,56},{56,64},{64,7... | collective-permute-start | bytes 3145736 | tf_op jit(solution)/shard_map/ppermute | solution.py:237

commit v2 on v1

v2 whole, which is shorter than its diff:
```python
import functools
import math

import jax
import jax.numpy as jnp
from jax import lax
from jax.experimental import pallas as pl
from jax.experimental.pallas import tpu as pltpu
from jax.sharding import PartitionSpec as P

CH = 512
START = 1024
RADIX = 4
LANES = 128
NT = (((1,), (1,)), ((), ()))
TN = (((0,), (0,)), ((), ()))
PLACES = ((0, 1), (4, 6), (2, 3), (7, 5))


def unit_roots(phase, frame_len):
    angle = (phase % frame_len).astype(jnp.float32) * jnp.float32(2.0 * math.pi / frame_len)
    return jnp.cos(angle), -jnp.sin(angle)


def turned(first, second):
    return first[0] * second[0] - first[1] * second[1], first[1] * second[0] + first[0] * second[1]


def table_kernel(frame_len, out):
    _, rows, span = out.shape
    shape = (rows, LANES)
    channel = pl.program_id(0) * rows + lax.broadcasted_iota(jnp.int32, shape, 0)
    column = lax.broadcasted_iota(jnp.int32, shape, 1)
    fine = unit_roots(RADIX * channel * column, frame_len)
    advance = unit_roots(RADIX * LANES * channel, frame_len)
    residue = lax.broadcasted_iota(jnp.int32, (8, LANES), 0)
    base = unit_roots((START + residue) * lax.broadcasted_iota(jnp.int32, (8, LANES), 1), frame_len)
    for res in range(RADIX):
        value = turned(fine, tuple(part[res : res + 1, :] for part in base))
        angle = 2.0 * math.pi * (LANES * (START + res) % frame_len) / frame_len
        turn = turned(advance, (jnp.float32(math.cos(angle)), jnp.float32(-math.sin(angle))))
        cosine, sine = PLACES[res]
        for start in range(0, span, LANES):
            out[cosine, :, start : start + LANES] = value[0].astype(jnp.bfloat16)
            out[sine, :, start : start + LANES] = value[1].astype(jnp.bfloat16)
            value = turned(value, turn)


def twiddles(frame_len):
    span = frame_len // RADIX
    quarter = CH // RADIX
    rows = 16
    table = pl.pallas_call(
        functools.partial(table_kernel, frame_len),
        grid=(quarter // rows,),
        out_specs=pl.BlockSpec((2 * RADIX, rows, span), lambda i: (0, i, 0)),
        out_shape=jax.ShapeDtypeStruct((2 * RADIX, quarter, span), jnp.bfloat16),
        name="twiddles",
    )()
    return table.reshape(2 * CH, span)


def spectra_kernel(tail, frames, width, batch, samples, taps, table, out, parts, sums_ref, wide):
    step = pl.program_id(0)
    taps_count = taps.shape[1]
    groups, low = samples.shape[0], samples.shape[2]
    in_dev = groups * low
    made = taps_count - 1 if tail else frames
    columns = frames * in_dev

    @pl.when(step == 0)
    def _():
        sums_ref[...] = jnp.zeros_like(sums_ref)
        if tail:
            parts[...] = jnp.zeros_like(parts)

    base = step % batch * width
    for lane in range(width // LANES):
        lanes = slice(lane * LANES, (lane + 1) * LANES)
        places = pl.ds(pl.multiple_of(base + lane * LANES, LANES), LANES)
        for b in range(RADIX):
            for t in range(taps_count):
                wide[lane % 2, b, t] = jnp.broadcast_to(taps[b, t : t + 1, lanes], (low, LANES))
        for group in range(groups):
            sums = []
            for b in (0, 2, 1, 3):
                block = [samples[group, n * RADIX + b, :, lanes].astype(jnp.float32) for n in range(frames)]
                totals = [None] * made
                for t in range(taps_count):
                    weight = wide[lane % 2, b, t]
                    for m in range(made):
                        n = frames + m - t if tail else m - t
                        if 0 <= n < frames:
                            term = weight * block[n]
                            totals[m] = term if totals[m] is None else totals[m] + term
                sums.append(totals)
                if b < 2:
                    continue
                second, first = sums.pop(), sums.pop()
                for m in range(made):
                    rows = slice(m * in_dev + group * low, m * in_dev + (group + 1) * low)
                    parts[b, rows, places] = first[m] - second[m]
                    first[m] = first[m] + second[m]
                    if b == 3:
                        parts[0, rows, places] = sums[0][m] + first[m]
                        parts[1, rows, places] = sums[0][m] - first[m]
                sums.append(first)

    quarter = table.shape[0] // (2 * RADIX)

    def product(block, part, negative=False):
        rows = table[2 * block * quarter : 2 * (block + 1) * quarter, :]
        rows = -rows if negative else rows
        return lax.dot_general(rows, parts[part], NT, preferred_element_type=jnp.float32)

    @pl.when(step % batch == batch - 1)
    def _():
        sums_ref[0] += product(0, 0)
        sums_ref[1] += product(1, 1)
        sums_ref[2] += product(2, 2) + product(3, 3)
        sums_ref[3] += product(3, 2) + product(2, 3, True)

    @pl.when(step == pl.num_programs(0) - 1)
    def _():
        scale = jnp.float32(1.0 / math.sqrt(RADIX * width * pl.num_programs(0)))
        tiles = columns // LANES
        height = 2 * RADIX * tiles
        order = ((0, 0), (0, 1), (2, 0), (3, 0), (1, 0), (1, 1), (3, 1), (2, 1))
        for start in range(0, quarter, 8):
            pieces = [
                sums_ref[block, part * quarter + start : part * quarter + start + 8, tile * LANES : (tile + 1) * LANES]
                for block, part in order
                for tile in range(tiles)
            ]
            value = jnp.transpose(jnp.stack(pieces), (1, 0, 2)) * scale
            out[start : start + 8] = value.astype(out.dtype)


def frame_spectra(voltages, taps, table, tail, width=512, batch=2):
    in_dev, length = voltages.shape
    tap_count, frame_len = taps.shape
    frames = length // frame_len
    span = frame_len // RADIX
    quarter = CH // RADIX
    columns = frames * in_dev

    low = 8
    samples = voltages.reshape(in_dev // low, low, frames * RADIX, span)
    samples = jnp.transpose(samples, (0, 2, 1, 3))
    taps = jnp.transpose(taps.reshape(tap_count, RADIX, span), (1, 0, 2))
    in_specs = [
        pl.BlockSpec((in_dev // low, frames * RADIX, low, width), lambda i: (0, 0, 0, i)),
        pl.BlockSpec((RADIX, tap_count, width), lambda i: (0, 0, i)),
        pl.BlockSpec((2 * CH, batch * width), lambda i: (0, i // batch)),
    ]
    height = 2 * RADIX * (columns // LANES)
    return pl.pallas_call(
        functools.partial(spectra_kernel, tail, frames, width, batch),
        grid=(span // width,),
        in_specs=in_specs,
        out_specs=pl.BlockSpec((quarter, height, LANES), lambda i: (0, 0, 0)),
        out_shape=jax.ShapeDtypeStruct((quarter, height, LANES), jnp.bfloat16 if tail else jnp.float32),
        scratch_shapes=[
            pltpu.VMEM((RADIX, columns, batch * width), jnp.float32),
            pltpu.VMEM((RADIX, 2 * quarter, columns), jnp.float32),
            pltpu.VMEM((2, RADIX, tap_count, low, LANES), jnp.float32),
        ],
        compiler_params=pltpu.CompilerParams(vmem_limit_bytes=50 * 2**20),
        cost_estimate=pl.CostEstimate(
            flops=2 * columns * 6 * quarter * 2 * span, bytes_accessed=26 * 2**20, transcendentals=0
        ),
        name="tail_spectra" if tail else "main_spectra",
    )(samples, taps, table)


def visibility_kernel(tm_count, inp_count, total_frames, block, out, left, right):
    lane = lax.broadcasted_iota(jnp.int32, (tm_count, 8, LANES), 2)
    row = lax.broadcasted_iota(jnp.int32, (tm_count, 8, LANES), 1)
    low = lane < LANES // 2
    real_row = row < 4
    half_depth = tm_count * 8
    scale = jnp.float32(1.0 / total_frames)
    for channel in range(block.shape[1] // 8):
        values = block[...].astype(jnp.float32)[:, channel * 8 : channel * 8 + 8, :]
        values = values.reshape(tm_count, inp_count, 8, LANES)
        for pair in range(inp_count // 2):
            first, second = values[:, 2 * pair], values[:, 2 * pair + 1]
            merged = (
                jnp.where(low, first, pltpu.roll(second, LANES // 2, 2)),
                jnp.where(low, pltpu.roll(first, LANES // 2, 2), second),
            )
            lanes = slice(pair * LANES, (pair + 1) * LANES)
            for part in range(2):
                rows = slice(part * half_depth, (part + 1) * half_depth)
                swapped = pltpu.roll(merged[part], 4, 1)
                swapped = jnp.where(real_row, -swapped, swapped)
                left[rows, lanes] = merged[part].reshape(half_depth, LANES).astype(jnp.bfloat16)
                right[rows, lanes] = swapped.reshape(half_depth, LANES).astype(jnp.bfloat16)
        out[channel, 0] = (
            lax.dot_general(left[...], left[...], TN, preferred_element_type=jnp.float32) * scale
        )
        out[channel, 1] = (
            lax.dot_general(left[...], right[...], TN, preferred_element_type=jnp.float32) * scale
        )


def visibilities(spectra, tm_count, inp_count, total_frames, inputs_all):
    devices, height, _ = spectra.shape
    per_device = CH // devices
    depth = 2 * tm_count * 8
    return pl.pallas_call(
        functools.partial(visibility_kernel, tm_count, inp_count, total_frames),
        grid=(height // 16,),
        in_specs=[pl.BlockSpec((devices, 16, LANES), lambda i: (0, i, 0))],
        out_specs=pl.BlockSpec((2, 2, inputs_all, inputs_all), lambda i: (i, 0, 0, 0)),
        out_shape=jax.ShapeDtypeStruct((per_device, 2, inputs_all, inputs_all), jnp.float32),
        scratch_shapes=[
            pltpu.VMEM((depth, inputs_all), jnp.bfloat16),
            pltpu.VMEM((depth, inputs_all), jnp.bfloat16),
        ],
        compiler_params=pltpu.CompilerParams(vmem_limit_bytes=50 * 2**20),
        name="visibilities",
    )(spectra)


def on_device(voltages, taps):
    in_dev, samples = voltages.shape
    frame_len = taps.shape[1]
    frames_dev = samples // frame_len
    tm_count, inp_count = lax.axis_size("tm"), lax.axis_size("inp")
    devices = tm_count * inp_count
    table = twiddles(frame_len)
    tail = frame_spectra(voltages, taps, table, True)
    tail, table, voltages = lax.optimization_barrier((tail, table, voltages))
    carried = lax.ppermute(tail, "tm", [(i, i + 1) for i in range(tm_count - 1)])
    main = frame_spectra(voltages, taps, table, False)
    spectra = (main + carried.astype(jnp.float32)).astype(jnp.bfloat16)
    spectra = spectra.reshape(devices, -1, LANES)
    spectra = lax.all_to_all(spectra, ("tm", "inp"), split_axis=0, concat_axis=0, tiled=True)
    return visibilities(spectra, tm_count, inp_count, tm_count * frames_dev, inp_count * in_dev)


def solution(mesh):
    return jax.shard_map(
        on_device,
        mesh=mesh,
        in_specs=(P("inp", "tm"), P()),
        out_specs=P(("tm", "inp"), None, None, None),
        check_vma=False,
    )
```

time: 100 us -> 88.6 us (0.89)
  Pallas kernels: 59.6 us -> 54.1 us
  local copies, waits for them, and re-layouts: 3.98 us -> 0.01 us
  other arithmetic: 2.35 us -> 0.32 us
    pallas_call x3, Pallas kernels: 55.1 us -> 49.5 us  [the longest x2 43.7 us: frame_spectra(): pl.pallas_call(functools.partial(spectra_kernel, tail, frames, width, bat...]
    reshape x4 -> x0, local copies, waits for them, and re-layouts: 3.98 us -> none  [twiddles(): part.reshape(CH, steps, groups)]
    sin x3 -> x0, other arithmetic: 2.05 us -> none  [unit_roots(): return (jnp.cos(angle), jnp.sin(angle))]
  transfers between devices with their start and end apart: 1 -> 1, of which waited for: 0 -> 0; matrix products, arithmetic and copies ran while one was open for 0% -> 0% of each run, Pallas kernels for 24% -> 25%
where the time goes in v2:
time: 88.6 us; the launch traced here: 88.3 us
  Pallas kernels  54.1 us (61%)
  blocking collectives  29.4 us (33%)
  starting transfers between devices  4.51 us (5%)
    pallas_call x2, Pallas kernels, frame_spectra(): pl.pallas_call(functools.partial(spectra_kernel, tail, frames, width, bat...  43.7 us
    all_to_all x1, blocking collectives, on_device(): lax.all_to_all(spectra, ('tm', 'inp'), split_axis=0, concat_axis=0, tiled...  29.4 us
    pallas_call x1, Pallas kernels, twiddles(): pl.pallas_call(functools.partial(table_kernel, frame_len), grid=(quarter...  5.87 us
    pallas_call x1, Pallas kernels, visibilities(): pl.pallas_call(functools.partial(visibility_kernel, tm_count, inp_count,...  4.52 us
    ppermute x1, starting transfers between devices, on_device(): lax.ppermute(tail, 'tm', [(i, i + 1) for i in range(tm_count - 1)])  4.51 us
  transfers between devices with their start and end apart: 1, of which 0 were waited for; matrix products, arithmetic and copies ran while one was open for 0% of the time, Pallas kernels for 25%

profile of v2, /device:TPU:1, one launch (start us, length us, event | category | flops | bytes accessed | tf_op | source)
XLA Modules:
  0.0 88.3 jit_solution(520854701513694074)
XLA Ops:
  0.0 0.0 copy-start
  0.0 5.9 %twiddles.1 = bf16[8,128,4096]{2,1,0:T(8,128)(2,1)} custom-call(), custom_call_target="tpu_custom_call" | custom-call | tf_op jit(solution)/shard_map/twiddles/pallas_call | solution.py:53
  5.9 0.0 copy-done
  5.9 21.6 %tail_spectra.1 = bf16[128,32,128]{2,1,0:T(8,128)(2,1)S(1)} custom-call(bf16[8,32,8,4096]{3,2,1,0:T(8,128)(2,1)} %bitcast.14, f32[4,8,4096]{2,1,0:T(8,128)S(1)} %bitcast.10, bf16[1024,4096]{1,0:T(8,128)(2,1)} %bitcast.12), custom_call_target="tpu_custom_call" | custom-call | flops 6442450944 | bytes 27262976 | tf_op jit(solution)/shard_map/tail_spectra/pallas_call | solution.py:157
  27.4 4.5 %collective-permute-start = (bf16[128,32,128]{2,1,0:T(8,128)(2,1)S(1)}, bf16[128,32,128]{2,1,0:T(8,128)(2,1)S(1)}, u32[]{:S(2)}, u32[]{:S(2)}) collective-permute-start(bf16[128,32,128]{2,1,0:T(8,128)(2,1)S(1)} %tail_spectra.1), channel_id=1, source_target_pairs={{0,8},{8,16},{16,24},{24,32},{32,40},{40,48},{48,56},{56,64},{64,7... | collective-permute-start | bytes 3145736 | tf_op jit(solution)/shard_map/ppermute | solution.py:235
  32.0 22.1 %main_spectra.1 = f32[128,32,128]{2,1,0:T(8,128)S(1)} custom-call(bf16[8,32,8,4096]{3,2,1,0:T(8,128)(2,1)} %bitcast.15, f32[4,8,4096]{2,1,0:T(8,128)S(1)} %bitcast.11, bf16[1024,4096]{1,0:T(8,128)(2,1)} %bitcast.13), custom_call_target="tpu_custom_call" | custom-call | flops 6442450944 | bytes 27262976 | tf_op jit(solution)/shard_map/main_spectra/pallas_call | solution.py:157
  54.1 0.0 collective-permute-done
  54.1 0.3 add_convert_fusion
  54.4 29.4 %all_to_all.5.block = bf16[128,32,128]{2,1,0:T(8,128)(2,1)S(1)} all-to-all(bf16[128,32,128]{2,1,0:T(8,128)(2,1)S(1)} %add_convert_fusion), channel_id=1, replica_groups=mesh['tm'=16,'inp'=8] {'tm','inp'}, dimensions={0} | all-to-all | bytes 2097152 | tf_op jit(solution)/shard_map/all_to_all | solution.py:239
  83.8 4.5 %visibilities.1 = f32[4,2,512,512]{3,2,1,0:T(8,128)} custom-call(bf16[128,32,128]{2,1,0:T(8,128)(2,1)S(1)} %all_to_all.5.block), custom_call_target="tpu_custom_call" | custom-call | tf_op jit(solution)/shard_map/visibilities/pallas_call | solution.py:211
Async XLA Ops:
  0.0 5.9 %copy-start = (f32[8,16384]{1,0:T(8,128)S(1)}, f32[8,16384]{1,0:T(8,128)}, u32[]{:S(2)}) copy-start(f32[8,16384]{1,0:T(8,128)} %param.3) | copy-start | bytes 1572868
  27.4 26.6 %collective-permute-start = (bf16[128,32,128]{2,1,0:T(8,128)(2,1)S(1)}, bf16[128,32,128]{2,1,0:T(8,128)(2,1)S(1)}, u32[]{:S(2)}, u32[]{:S(2)}) collective-permute-start(bf16[128,32,128]{2,1,0:T(8,128)(2,1)S(1)} %tail_spectra.1), channel_id=1, source_target_pairs={{0,8},{8,16},{16,24},{24,32},{32,40},{40,48},{48,56},{56,64},{64,7... | collective-permute-start | bytes 3145736 | tf_op jit(solution)/shard_map/ppermute | solution.py:235

commit v3 on v2

--- a/solution.py
+++ b/solution.py
@@ -10,11 +10,14 @@
 
 CH = 512
 START = 1024
-RADIX = 4
+RADIX = 8
 LANES = 128
 NT = (((1,), (1,)), ((), ()))
 TN = (((0,), (0,)), ((), ()))
-PLACES = ((0, 1), (4, 6), (2, 3), (7, 5))
+PAIRS = ((1, 7), (2, 6), (3, 5))
+TABLE_PARTS = 4 + 6 * len(PAIRS)
+EVEN_ORDER = (0, 1, 4, 6, 8, 10, 12, 14)
+ODD_ORDER = (2, 3, 15, 13, 11, 9, 7, 5)
 
 
 def unit_roots(phase, frame_len):
@@ -24,6 +27,17 @@
 
 def turned(first, second):
     return first[0] * second[0] - first[1] * second[1], first[1] * second[0] + first[0] * second[1]
+
+
+def table_places(res):
+    if res % 4 == 0:
+        return ((res // 2, False),), ((res // 2 + 1, False),)
+    for index, (lead, mirror) in enumerate(PAIRS):
+        start = 4 + 6 * index
+        if res == lead:
+            return ((start, False), (start + 4, True)), ((start + 2, False),)
+        if res == mirror:
+            return ((start + 3, False),), ((start + 1, False), (start + 5, True))
 
 
 def table_kernel(frame_len, out):
@@ -33,31 +47,33 @@
     column = lax.broadcasted_iota(jnp.int32, shape, 1)
     fine = unit_roots(RADIX * channel * column, frame_len)
     advance = unit_roots(RADIX * LANES * channel, frame_len)
-    residue = lax.broadcasted_iota(jnp.int32, (8, LANES), 0)
-    base = unit_roots((START + residue) * lax.broadcasted_iota(jnp.int32, (8, LANES), 1), frame_len)
+    residue = lax.broadcasted_iota(jnp.int32, (RADIX, LANES), 0)
+    base = unit_roots((START + residue) * lax.broadcasted_iota(jnp.int32, (RADIX, LANES), 1), frame_len)
     for res in range(RADIX):
         value = turned(fine, tuple(part[res : res + 1, :] for part in base))
         angle = 2.0 * math.pi * (LANES * (START + res) % frame_len) / frame_len
         turn = turned(advance, (jnp.float32(math.cos(angle)), jnp.float32(-math.sin(angle))))
-        cosine, sine = PLACES[res]
+        places = table_places(res)
         for start in range(0, span, LANES):
-            out[cosine, :, start : start + LANES] = value[0].astype(jnp.bfloat16)
-            out[sine, :, start : start + LANES] = value[1].astype(jnp.bfloat16)
+            for which in range(2):
+                entry = value[which].astype(jnp.bfloat16)
+                for part, negated in places[which]:
+                    out[part, :, start : start + LANES] = -entry if negated else entry
             value = turned(value, turn)
 
 
 def twiddles(frame_len):
     span = frame_len // RADIX
-    quarter = CH // RADIX
+    eighth = CH // RADIX
     rows = 16
     table = pl.pallas_call(
         functools.partial(table_kernel, frame_len),
-        grid=(quarter // rows,),
-        out_specs=pl.BlockSpec((2 * RADIX, rows, span), lambda i: (0, i, 0)),
-        out_shape=jax.ShapeDtypeStruct((2 * RADIX, quarter, span), jnp.bfloat16),
+        grid=(eighth // rows,),
+        out_specs=pl.BlockSpec((TABLE_PARTS, rows, span), lambda i: (0, i, 0)),
+        out_shape=jax.ShapeDtypeStruct((TABLE_PARTS, eighth, span), jnp.bfloat16),
         name="twiddles",
     )()
-    return table.reshape(2 * CH, span)
+    return table.reshape(TABLE_PARTS * eighth, span)
 
 
 def spectra_kernel(tail, frames, width, batch, samples, taps, table, out, parts, sums_ref, wide):
@@ -82,66 +98,75 @@
             for t in range(taps_count):
                 wide[lane % 2, b, t] = jnp.broadcast_to(taps[b, t : t + 1, lanes], (low, LANES))
         for group in range(groups):
-            sums = []
-            for b in (0, 2, 1, 3):
-                block = [samples[group, n * RADIX + b, :, lanes].astype(jnp.float32) for n in range(frames)]
-                totals = [None] * made
-                for t in range(taps_count):
-                    weight = wide[lane % 2, b, t]
-                    for m in range(made):
-                        n = frames + m - t if tail else m - t
-                        if 0 <= n < frames:
-                            term = weight * block[n]
-                            totals[m] = term if totals[m] is None else totals[m] + term
-                sums.append(totals)
-                if b < 2:
-                    continue
-                second, first = sums.pop(), sums.pop()
-                for m in range(made):
-                    rows = slice(m * in_dev + group * low, m * in_dev + (group + 1) * low)
-                    parts[b, rows, places] = first[m] - second[m]
-                    first[m] = first[m] + second[m]
-                    if b == 3:
-                        parts[0, rows, places] = sums[0][m] + first[m]
-                        parts[1, rows, places] = sums[0][m] - first[m]
-                sums.append(first)
-
-    quarter = table.shape[0] // (2 * RADIX)
-
-    def product(block, part, negative=False):
-        rows = table[2 * block * quarter : 2 * (block + 1) * quarter, :]
-        rows = -rows if negative else rows
+            kept = []
+            for first in (0, 2, 1, 3):
+                pair = []
+                for b in (first, first + 4):
+                    block = [samples[group, n * RADIX + b, :, lanes].astype(jnp.float32) for n in range(frames)]
+                    totals = [None] * made
+                    for t in range(taps_count):
+                        weight = wide[lane % 2, b, t]
+                        for m in range(made):
+                            n = frames + m - t if tail else m - t
+                            if 0 <= n < frames:
+                                term = weight * block[n]
+                                totals[m] = term if totals[m] is None else totals[m] + term
+                    pair.append(totals)
+                kept.append(([x + y for x, y in zip(*pair)], [x - y for x, y in zip(*pair)]))
+            (s0, d0), (s2, d2), (s1, d1), (s3, d3) = kept
+            root = jnp.float32(math.sqrt(0.5))
+            for m in range(made):
+                rows = slice(m * in_dev + group * low, m * in_dev + (group + 1) * low)
+                even, odd = s0[m] + s2[m], s1[m] + s3[m]
+                across, along = (d1[m] - d3[m]) * root, (d1[m] + d3[m]) * root
+                parts[0, rows, places] = even + odd
+                parts[1, rows, places] = even - odd
+                parts[2, rows, places] = d0[m] + across
+                parts[3, rows, places] = along + d2[m]
+                parts[4, rows, places] = s0[m] - s2[m]
+                parts[5, rows, places] = s1[m] - s3[m]
+                parts[6, rows, places] = d0[m] - across
+                parts[7, rows, places] = along - d2[m]
+
+    eighth = table.shape[0] // TABLE_PARTS
+
+    def product(first, last, part):
+        rows = table[first * eighth : last * eighth, :]
         return lax.dot_general(rows, parts[part], NT, preferred_element_type=jnp.float32)
 
     @pl.when(step % batch == batch - 1)
     def _():
-        sums_ref[0] += product(0, 0)
-        sums_ref[1] += product(1, 1)
-        sums_ref[2] += product(2, 2) + product(3, 3)
-        sums_ref[3] += product(3, 2) + product(2, 3, True)
+        sums_ref[: 2 * eighth] += product(0, 2, 0)
+        sums_ref[2 * eighth : 4 * eighth] += product(2, 4, 1)
+        for index in range(len(PAIRS)):
+            rows = slice((4 + 4 * index) * eighth, (8 + 4 * index) * eighth)
+            first = 4 + 6 * index
+            sums_ref[rows] += product(first, first + 4, 2 + 2 * index) + product(first + 2, first + 6, 3 + 2 * index)
 
     @pl.when(step == pl.num_programs(0) - 1)
     def _():
         scale = jnp.float32(1.0 / math.sqrt(RADIX * width * pl.num_programs(0)))
         tiles = columns // LANES
         height = 2 * RADIX * tiles
-        order = ((0, 0), (0, 1), (2, 0), (3, 0), (1, 0), (1, 1), (3, 1), (2, 1))
-        for start in range(0, quarter, 8):
-            pieces = [
-                sums_ref[block, part * quarter + start : part * quarter + start + 8, tile * LANES : (tile + 1) * LANES]
-                for block, part in order
-                for tile in range(tiles)
-            ]
-            value = jnp.transpose(jnp.stack(pieces), (1, 0, 2)) * scale
-            out[start : start + 8] = value.astype(out.dtype)
-
-
-def frame_spectra(voltages, taps, table, tail, width=512, batch=2):
+        for start in range(0, eighth, 8):
+            both = []
+            for order in (EVEN_ORDER, ODD_ORDER):
+                pieces = [
+                    sums_ref[part * eighth + start : part * eighth + start + 8, tile * LANES : (tile + 1) * LANES]
+                    for part in order
+                    for tile in range(tiles)
+                ]
+                both.append(jnp.transpose(jnp.stack(pieces), (1, 0, 2)) * scale)
+            value = jnp.stack(both, axis=1).reshape(16, len(pieces), LANES)
+            out[2 * start : 2 * start + 16] = value.astype(out.dtype)
+
+
+def frame_spectra(voltages, taps, table, tail, width=256, batch=4):
     in_dev, length = voltages.shape
     tap_count, frame_len = taps.shape
     frames = length // frame_len
     span = frame_len // RADIX
-    quarter = CH // RADIX
+    devices = CH // 4
     columns = frames * in_dev
 
     low = 8
@@ -151,23 +176,23 @@
     in_specs = [
         pl.BlockSpec((in_dev // low, frames * RADIX, low, width), lambda i: (0, 0, 0, i)),
         pl.BlockSpec((RADIX, tap_count, width), lambda i: (0, 0, i)),
-        pl.BlockSpec((2 * CH, batch * width), lambda i: (0, i // batch)),
+        pl.BlockSpec((table.shape[0], batch * width), lambda i: (0, i // batch)),
     ]
-    height = 2 * RADIX * (columns // LANES)
+    height = 8 * (columns // LANES)
     return pl.pallas_call(
         functools.partial(spectra_kernel, tail, frames, width, batch),
         grid=(span // width,),
         in_specs=in_specs,
-        out_specs=pl.BlockSpec((quarter, height, LANES), lambda i: (0, 0, 0)),
-        out_shape=jax.ShapeDtypeStruct((quarter, height, LANES), jnp.bfloat16 if tail else jnp.float32),
+        out_specs=pl.BlockSpec((devices, height, LANES), lambda i: (0, 0, 0)),
+        out_shape=jax.ShapeDtypeStruct((devices, height, LANES), jnp.bfloat16 if tail else jnp.float32),
         scratch_shapes=[
             pltpu.VMEM((RADIX, columns, batch * width), jnp.float32),
-            pltpu.VMEM((RADIX, 2 * quarter, columns), jnp.float32),
+            pltpu.VMEM((2 * CH, columns), jnp.float32),
             pltpu.VMEM((2, RADIX, tap_count, low, LANES), jnp.float32),
         ],
         compiler_params=pltpu.CompilerParams(vmem_limit_bytes=50 * 2**20),
         cost_estimate=pl.CostEstimate(
-            flops=2 * columns * 6 * quarter * 2 * span, bytes_accessed=26 * 2**20, transcendentals=0
+            flops=2 * columns * (7 * CH // 2) * span, bytes_accessed=26 * 2**20, transcendentals=0
         ),
         name="tail_spectra" if tail else "main_spectra",
     )(samples, taps, table)

time: 88.6 us -> 85.9 us (0.970)
  Pallas kernels: 54.1 us -> 51.4 us
    pallas_call x1, Pallas kernels: 5.87 us -> 3.58 us  [twiddles(): pl.pallas_call(functools.partial(table_kernel, frame_len), grid=(eighth /...]
  transfers between devices with their start and end apart: 1 -> 1, of which waited for: 0 -> 0; matrix products, arithmetic and copies ran while one was open for 0% -> 0% of each run, Pallas kernels for 25% -> 26%
where the time goes in v3:
time: 85.9 us; the launch traced here: 85.6 us
  Pallas kernels  51.4 us (60%)
  blocking collectives  29.4 us (34%)
  starting transfers between devices  4.52 us (5%)
    pallas_call x2, Pallas kernels, frame_spectra(): pl.pallas_call(functools.partial(spectra_kernel, tail, frames, width, bat...  43.3 us
    all_to_all x1, blocking collectives, on_device(): lax.all_to_all(spectra, ('tm', 'inp'), split_axis=0, concat_axis=0, tiled...  29.4 us
    pallas_call x1, Pallas kernels, visibilities(): pl.pallas_call(functools.partial(visibility_kernel, tm_count, inp_count,...  4.52 us
    ppermute x1, starting transfers between devices, on_device(): lax.ppermute(tail, 'tm', [(i, i + 1) for i in range(tm_count - 1)])  4.52 us
    pallas_call x1, Pallas kernels, twiddles(): pl.pallas_call(functools.partial(table_kernel, frame_len), grid=(eighth /...  3.58 us
  transfers between devices with their start and end apart: 1, of which 0 were waited for; matrix products, arithmetic and copies ran while one was open for 0% of the time, Pallas kernels for 26%

profile of v3, /device:TPU:1, one launch (start us, length us, event | category | flops | bytes accessed | tf_op | source)
XLA Modules:
  0.0 85.6 jit_solution(1809306684930605691)
XLA Ops:
  0.0 0.0 copy-start
  0.0 3.6 %twiddles.1 = bf16[22,64,2048]{2,1,0:T(8,128)(2,1)} custom-call(), custom_call_target="tpu_custom_call" | custom-call | tf_op jit(solution)/shard_map/twiddles/pallas_call | solution.py:69
  3.6 0.0 copy-done
  3.6 21.1 %tail_spectra.1 = bf16[128,32,128]{2,1,0:T(8,128)(2,1)S(1)} custom-call(bf16[8,64,8,2048]{3,2,1,0:T(8,128)(2,1)} %bitcast.12, f32[8,8,2048]{2,1,0:T(8,128)S(1)} %bitcast.10, bf16[1408,2048]{1,0:T(8,128)(2,1)} %bitcast.14), custom_call_target="tpu_custom_call" | custom-call | flops 3758096384 | bytes 27262976 | tf_op jit(solution)/shard_map/tail_spectra/pallas_call | solution.py:182
  24.7 4.5 %collective-permute-start = (bf16[128,32,128]{2,1,0:T(8,128)(2,1)S(1)}, bf16[128,32,128]{2,1,0:T(8,128)(2,1)S(1)}, u32[]{:S(2)}, u32[]{:S(2)}) collective-permute-start(bf16[128,32,128]{2,1,0:T(8,128)(2,1)S(1)} %tail_spectra.1), channel_id=1, source_target_pairs={{0,8},{8,16},{16,24},{24,32},{32,40},{40,48},{48,56},{56,64},{64,7... | collective-permute-start | bytes 3145736 | tf_op jit(solution)/shard_map/ppermute | solution.py:260
  29.2 22.2 %main_spectra.1 = f32[128,32,128]{2,1,0:T(8,128)S(1)} custom-call(bf16[8,64,8,2048]{3,2,1,0:T(8,128)(2,1)} %bitcast.13, f32[8,8,2048]{2,1,0:T(8,128)S(1)} %bitcast.11, bf16[1408,2048]{1,0:T(8,128)(2,1)} %bitcast.15), custom_call_target="tpu_custom_call" | custom-call | flops 3758096384 | bytes 27262976 | tf_op jit(solution)/shard_map/main_spectra/pallas_call | solution.py:182
  51.4 0.0 collective-permute-done
  51.4 0.3 add_convert_fusion
  51.7 29.4 %all_to_all.5.block = bf16[128,32,128]{2,1,0:T(8,128)(2,1)S(1)} all-to-all(bf16[128,32,128]{2,1,0:T(8,128)(2,1)S(1)} %add_convert_fusion), channel_id=1, replica_groups=mesh['tm'=16,'inp'=8] {'tm','inp'}, dimensions={0} | all-to-all | bytes 2097152 | tf_op jit(solution)/shard_map/all_to_all | solution.py:264
  81.1 4.5 %visibilities.1 = f32[4,2,512,512]{3,2,1,0:T(8,128)} custom-call(bf16[128,32,128]{2,1,0:T(8,128)(2,1)S(1)} %all_to_all.5.block), custom_call_target="tpu_custom_call" | custom-call | tf_op jit(solution)/shard_map/visibilities/pallas_call | solution.py:236
Async XLA Ops:
  0.0 3.6 %copy-start = (f32[8,16384]{1,0:T(8,128)S(1)}, f32[8,16384]{1,0:T(8,128)}, u32[]{:S(2)}) copy-start(f32[8,16384]{1,0:T(8,128)} %param.3) | copy-start | bytes 1572868
  24.7 26.7 %collective-permute-start = (bf16[128,32,128]{2,1,0:T(8,128)(2,1)S(1)}, bf16[128,32,128]{2,1,0:T(8,128)(2,1)S(1)}, u32[]{:S(2)}, u32[]{:S(2)}) collective-permute-start(bf16[128,32,128]{2,1,0:T(8,128)(2,1)S(1)} %tail_spectra.1), channel_id=1, source_target_pairs={{0,8},{8,16},{16,24},{24,32},{32,40},{40,48},{48,56},{56,64},{64,7... | collective-permute-start | bytes 3145736 | tf_op jit(solution)/shard_map/ppermute | solution.py:260

commit v4 on v3

--- a/solution.py
+++ b/solution.py
@@ -76,7 +76,7 @@
     return table.reshape(TABLE_PARTS * eighth, span)
 
 
-def spectra_kernel(tail, frames, width, batch, samples, taps, table, out, parts, sums_ref, wide):
+def spectra_kernel(tail, frames, width, batch, samples, taps, source, out, parts, sums_ref, wide, table, arrived):
     step = pl.program_id(0)
     taps_count = taps.shape[1]
     groups, low = samples.shape[0], samples.shape[2]
@@ -89,6 +89,13 @@
         sums_ref[...] = jnp.zeros_like(sums_ref)
         if tail:
             parts[...] = jnp.zeros_like(parts)
+
+    chunk = pl.ds(pl.multiple_of(step // batch * batch * width, batch * width), batch * width)
+    load = pltpu.make_async_copy(source.at[:, chunk], table, arrived)
+
+    @pl.when(step % batch == 0)
+    def _():
+        load.start()
 
     base = step % batch * width
     for lane in range(width // LANES):
@@ -136,6 +143,7 @@
 
     @pl.when(step % batch == batch - 1)
     def _():
+        load.wait()
         sums_ref[: 2 * eighth] += product(0, 2, 0)
         sums_ref[2 * eighth : 4 * eighth] += product(2, 4, 1)
         for index in range(len(PAIRS)):
@@ -176,7 +184,7 @@
     in_specs = [
         pl.BlockSpec((in_dev // low, frames * RADIX, low, width), lambda i: (0, 0, 0, i)),
         pl.BlockSpec((RADIX, tap_count, width), lambda i: (0, 0, i)),
-        pl.BlockSpec((table.shape[0], batch * width), lambda i: (0, i // batch)),
+        pl.BlockSpec(memory_space=pl.ANY),
     ]
     height = 8 * (columns // LANES)
     return pl.pallas_call(
@@ -189,6 +197,8 @@
             pltpu.VMEM((RADIX, columns, batch * width), jnp.float32),
             pltpu.VMEM((2 * CH, columns), jnp.float32),
             pltpu.VMEM((2, RADIX, tap_count, low, LANES), jnp.float32),
+            pltpu.VMEM((table.shape[0], batch * width), table.dtype),
+            pltpu.SemaphoreType.DMA,
         ],
         compiler_params=pltpu.CompilerParams(vmem_limit_bytes=50 * 2**20),
         cost_estimate=pl.CostEstimate(

time: 85.9 us -> 84.2 us (0.980)
  Pallas kernels: 51.4 us -> 49.7 us
    pallas_call x2, Pallas kernels: 43.3 us -> 41.6 us  [frame_spectra(): pl.pallas_call(functools.partial(spectra_kernel, tail, frames, width, bat...]
  transfers between devices with their start and end apart: 1 -> 1, of which waited for: 0 -> 0; matrix products, arithmetic and copies ran while one was open for 0% -> 0% of each run, Pallas kernels for 26% -> 25%
where the time goes in v4:
time: 84.2 us; the launch traced here: 84 us
  Pallas kernels  49.7 us (59%)
  blocking collectives  29.4 us (35%)
  starting transfers between devices  4.51 us (5%)
    pallas_call x2, Pallas kernels, frame_spectra(): pl.pallas_call(functools.partial(spectra_kernel, tail, frames, width, bat...  41.6 us
    all_to_all x1, blocking collectives, on_device(): lax.all_to_all(spectra, ('tm', 'inp'), split_axis=0, concat_axis=0, tiled...  29.4 us
    pallas_call x1, Pallas kernels, visibilities(): pl.pallas_call(functools.partial(visibility_kernel, tm_count, inp_count,...  4.52 us
    ppermute x1, starting transfers between devices, on_device(): lax.ppermute(tail, 'tm', [(i, i + 1) for i in range(tm_count - 1)])  4.51 us
    pallas_call x1, Pallas kernels, twiddles(): pl.pallas_call(functools.partial(table_kernel, frame_len), grid=(eighth /...  3.58 us
  transfers between devices with their start and end apart: 1, of which 0 were waited for; matrix products, arithmetic and copies ran while one was open for 0% of the time, Pallas kernels for 25%

profile of v4, /device:TPU:1, one launch (start us, length us, event | category | flops | bytes accessed | tf_op | source)
XLA Modules:
  0.0 84.0 jit_solution(15336457979680623742)
XLA Ops:
  0.0 0.0 copy-start
  0.0 3.6 %twiddles.1 = bf16[22,64,2048]{2,1,0:T(8,128)(2,1)} custom-call(), custom_call_target="tpu_custom_call" | custom-call | tf_op jit(solution)/shard_map/twiddles/pallas_call | solution.py:69
  3.6 0.0 copy-done
  3.6 20.4 %tail_spectra.1 = bf16[128,32,128]{2,1,0:T(8,128)(2,1)S(1)} custom-call(bf16[8,64,8,2048]{3,2,1,0:T(8,128)(2,1)} %bitcast.12, f32[8,8,2048]{2,1,0:T(8,128)S(1)} %bitcast.10, bf16[1408,2048]{1,0:T(8,128)(2,1)} %bitcast.14), custom_call_target="tpu_custom_call" | custom-call | flops 3758096384 | bytes 27262976 | tf_op jit(solution)/shard_map/tail_spectra/pallas_call | solution.py:190
  24.0 4.5 %collective-permute-start = (bf16[128,32,128]{2,1,0:T(8,128)(2,1)S(1)}, bf16[128,32,128]{2,1,0:T(8,128)(2,1)S(1)}, u32[]{:S(2)}, u32[]{:S(2)}) collective-permute-start(bf16[128,32,128]{2,1,0:T(8,128)(2,1)S(1)} %tail_spectra.1), channel_id=1, source_target_pairs={{0,8},{8,16},{16,24},{24,32},{32,40},{40,48},{48,56},{56,64},{64,7... | collective-permute-start | bytes 3145736 | tf_op jit(solution)/shard_map/ppermute | solution.py:270
  28.5 21.2 %main_spectra.1 = f32[128,32,128]{2,1,0:T(8,128)S(1)} custom-call(bf16[8,64,8,2048]{3,2,1,0:T(8,128)(2,1)} %bitcast.13, f32[8,8,2048]{2,1,0:T(8,128)S(1)} %bitcast.11, bf16[1408,2048]{1,0:T(8,128)(2,1)} %bitcast.15), custom_call_target="tpu_custom_call" | custom-call | flops 3758096384 | bytes 27262976 | tf_op jit(solution)/shard_map/main_spectra/pallas_call | solution.py:190
  49.7 0.0 collective-permute-done
  49.7 0.3 add_convert_fusion
  50.1 29.4 %all_to_all.5.block = bf16[128,32,128]{2,1,0:T(8,128)(2,1)S(1)} all-to-all(bf16[128,32,128]{2,1,0:T(8,128)(2,1)S(1)} %add_convert_fusion), channel_id=1, replica_groups=mesh['tm'=16,'inp'=8] {'tm','inp'}, dimensions={0} | all-to-all | bytes 2097152 | tf_op jit(solution)/shard_map/all_to_all | solution.py:274
  79.5 4.5 %visibilities.1 = f32[4,2,512,512]{3,2,1,0:T(8,128)} custom-call(bf16[128,32,128]{2,1,0:T(8,128)(2,1)S(1)} %all_to_all.5.block), custom_call_target="tpu_custom_call" | custom-call | tf_op jit(solution)/shard_map/visibilities/pallas_call | solution.py:246
Async XLA Ops:
  0.0 3.6 %copy-start = (f32[8,16384]{1,0:T(8,128)S(1)}, f32[8,16384]{1,0:T(8,128)}, u32[]{:S(2)}) copy-start(f32[8,16384]{1,0:T(8,128)} %param.3) | copy-start | bytes 1572868
  24.0 25.8 %collective-permute-start = (bf16[128,32,128]{2,1,0:T(8,128)(2,1)S(1)}, bf16[128,32,128]{2,1,0:T(8,128)(2,1)S(1)}, u32[]{:S(2)}, u32[]{:S(2)}) collective-permute-start(bf16[128,32,128]{2,1,0:T(8,128)(2,1)S(1)} %tail_spectra.1), channel_id=1, source_target_pairs={{0,8},{8,16},{16,24},{24,32},{32,40},{40,48},{48,56},{56,64},{64,7... | collective-permute-start | bytes 3145736 | tf_op jit(solution)/shard_map/ppermute | solution.py:270
